TPU v7x, 128 devices: a whole 4x4x4 slice. The times are simulated.
128 devices in a mesh: tx: 8 (over y, core), ty: 16 (over z, x).
Axes of the slice: x: 4, y: 4, z: 4, core: 2. Of those that a mesh axis runs over, the one named last changes fastest.
Arguments:
- probes: bfloat16 [512, 64, 2048], P(('tx', 'ty')), may hold values from -6 to 6
- points: float32 [512, 8, 2048], P(('tx', 'ty')), may hold values from 0 to 1
- up_basis: bfloat16 [512, 256, 2048], P(('tx', 'ty')), may hold values from -0.125 to 0.125
- down_basis: bfloat16 [512, 256, 2048], P(('tx', 'ty')), may hold values from -0.09375 to 0.09375
- box_skeleton: int32 [512, 256], P(('tx', 'ty')), may hold values from 0 to 2047, as said below
- box_transfer: bfloat16 [512, 256, 256], P(('tx', 'ty')), may hold values from -0.375 to 0.375
- node_skeleton: int32 [128, 256], P(('tx', 'ty')), may hold values from 0 to 1023, as said below
- node_transfer: bfloat16 [128, 256, 256], P(('tx', 'ty')), may hold values from -0.375 to 0.375
- group_skeleton: int32 [8, 256], replicated, may hold values from 0 to 4095, as said below
- near_list: int32 [512, 3], P(('tx', 'ty')), may hold values from -1 to 511, as said below
- node_list: int32 [128, 8], P(('tx', 'ty')), may hold values from 0 to 127, as said below
Outputs:
- applied: bfloat16 [512, 64, 2048], P(('tx', 'ty'))
Inputs may be any that keep to these rules, and one draw needn't show every extreme that they name: `box_skeleton`: each row names 256 distinct points of its box. `node_skeleton`: each row names 256 distinct points among the 1024 skeleton points of the node's boxes, numbered box by box. `group_skeleton`: each row names 256 distinct points among the 4096 skeleton points of the group's middle-level nodes, numbered node by node. `near_list`: box b of node d names 1 to 3 distinct boxes, live entries first and -1 after them; every named box belongs to d or to the nodes d - 1 and d + 1 where these lie in d's upper-level node. `node_list`: node d names 8 distinct nodes of its own upper-level node whose ty index differs from d's by two or more.
All inputs are finite; a program needn't handle non-finite values.
Results may differ from a plain program's by a relative error of at most 0.024.
Values may be sent and summed in bfloat16 or wider, within the bound.
No kernel may reach another device: no remote copies, remote signals or barrier semaphores. Data moves between devices by JAX's collectives and lax.ppermute only.
A program may use at most 128 MiB of HBM per device.

v0:
```python
import jax
import jax.numpy as jnp
from jax import lax
from jax.sharding import PartitionSpec as P

inv_length = 4.0


def with_halo(cells, sides, width):
    for axis, dim in sides:
        count = lax.axis_size(axis)
        ends = count - 1
        head = lax.slice_in_dim(cells, 0, width, axis=dim)
        tail = lax.slice_in_dim(cells, cells.shape[dim] - width, cells.shape[dim], axis=dim)
        cells = jnp.concatenate(
            [
                lax.ppermute(tail, axis, [(i, (i + 1) % count) for i in range(ends)]),
                cells,
                lax.ppermute(head, axis, [((i + 1) % count, i) for i in range(ends)]),
            ],
            axis=dim,
        )
    return cells


def kernel_block(source, target):
    squared = jnp.zeros((source.shape[1], target.shape[1]), jnp.float32)
    for feature in range(source.shape[0]):
        offset = source[feature][:, None] - target[feature][None, :]
        squared = squared + offset * offset
    scaled = jnp.sqrt(squared) * inv_length
    return (scaled * jnp.exp(-scaled)).astype(jnp.bfloat16)


def shards(
    probes,
    points,
    up_basis,
    down_basis,
    box_skeleton,
    box_transfer,
    node_skeleton,
    node_transfer,
    group_skeleton,
    near_list,
    node_list,
):
    boxes = probes.shape[0]
    probe_count = probes.shape[1]
    leaf_count = probes.shape[2]
    features = points.shape[1]
    rank = up_basis.shape[1]
    n_tx = lax.axis_size("tx")
    n_ty = lax.axis_size("ty")
    tx_index = lax.axis_index("tx")
    ty_index = lax.axis_index("ty")
    box_weights = jnp.einsum(
        "bql,brl->bqr", probes, up_basis, preferred_element_type=jnp.float32
    ).astype(jnp.bfloat16)
    node_weight = jnp.einsum(
        "bqr,brs->qs", box_weights, box_transfer, preferred_element_type=jnp.float32
    ).astype(jnp.bfloat16)
    index_box = jnp.broadcast_to(box_skeleton[:, None, :], (boxes, features, rank))
    box_points = jnp.take_along_axis(points, index_box, axis=2)
    pooled = jnp.transpose(box_points, (1, 0, 2)).reshape(features, boxes * rank)
    node_points = jnp.take(pooled, node_skeleton[0], axis=1)
    node_term = jnp.dot(node_weight, node_transfer[0], preferred_element_type=jnp.float32)
    ty_weights = lax.all_gather(node_weight[None], "ty", axis=0, tiled=True)
    ty_points = lax.all_gather(node_points[None], "ty", axis=0, tiled=True)
    group_weight = lax.psum(node_term.astype(jnp.bfloat16), "ty")
    ty_pooled = jnp.transpose(ty_points, (1, 0, 2)).reshape(features, n_ty * rank)
    own_skeleton = lax.dynamic_index_in_dim(group_skeleton, tx_index, 0, keepdims=False)
    own_group = jnp.take(ty_pooled, own_skeleton, axis=1)
    every_weight = lax.all_gather(group_weight[None], "tx", axis=0, tiled=True)
    every_points = lax.all_gather(own_group[None], "tx", axis=0, tiled=True)
    group_blocks = jax.vmap(kernel_block, in_axes=(0, None))(every_points, own_group)
    group_terms = jnp.einsum(
        "gqr,grs->gqs", every_weight, group_blocks, preferred_element_type=jnp.float32
    )
    keep_group = (jnp.arange(n_tx) != tx_index)[:, None, None]
    group_potential = jnp.sum(jnp.where(keep_group, group_terms, 0.0), axis=0).astype(jnp.bfloat16)
    local_nodes = node_list[0] - tx_index * n_ty
    far_weights = jnp.take(ty_weights, local_nodes, axis=0)
    far_points = jnp.take(ty_points, local_nodes, axis=0)
    far_blocks = jax.vmap(kernel_block, in_axes=(0, None))(far_points, node_points)
    far_sum = jnp.einsum("kqr,krs->qs", far_weights, far_blocks, preferred_element_type=jnp.float32)
    pushed = jnp.einsum(
        "qs,rs->qr", group_potential, node_transfer[0], preferred_element_type=jnp.float32
    )
    node_potential = (far_sum + pushed).astype(jnp.bfloat16)
    box_potential = jnp.einsum(
        "qs,brs->bqr", node_potential, box_transfer, preferred_element_type=jnp.float32
    ).astype(jnp.bfloat16)
    far_output = jnp.einsum(
        "bqr,brl->bql", box_potential, down_basis, preferred_element_type=jnp.float32
    )
    near_probes = with_halo(probes, (("ty", 0),), boxes)
    near_points = with_halo(points.astype(jnp.bfloat16), (("ty", 0),), boxes).astype(points.dtype)
    window_start = (tx_index * n_ty + ty_index) * boxes - boxes
    local_near = jnp.clip(near_list - window_start, 0, 3 * boxes - 1)
    live_near = near_list >= 0

    def near_tile(source_slot, own_points):
        source_probes = lax.dynamic_index_in_dim(near_probes, source_slot, 0, keepdims=False)
        source_points = lax.dynamic_index_in_dim(near_points, source_slot, 0, keepdims=False)
        return jnp.dot(
            source_probes,
            kernel_block(source_points, own_points),
            preferred_element_type=jnp.float32,
        )

    def near_box(box_index, accumulated):
        own_points = lax.dynamic_index_in_dim(points, box_index, 0, keepdims=False)
        slot_row = lax.dynamic_index_in_dim(local_near, box_index, 0, keepdims=False)
        live_row = lax.dynamic_index_in_dim(live_near, box_index, 0, keepdims=False)
        total = jnp.zeros((probe_count, leaf_count), jnp.float32)
        for entry in range(near_list.shape[1]):
            term = jnp.where(live_row[entry], near_tile(slot_row[entry], own_points), 0.0)
            total = total + term
        return lax.dynamic_update_index_in_dim(accumulated, total, box_index, 0)

    near_sum = lax.fori_loop(
        0, boxes, near_box, jnp.zeros((boxes, probe_count, leaf_count), jnp.float32)
    )
    return (far_output + near_sum).astype(jnp.bfloat16)


def solution(mesh):
    in_specs = (
        P(("tx", "ty"), None, None),
        P(("tx", "ty"), None, None),
        P(("tx", "ty"), None, None),
        P(("tx", "ty"), None, None),
        P(("tx", "ty"), None),
        P(("tx", "ty"), None, None),
        P(("tx", "ty"), None),
        P(("tx", "ty"), None, None),
        P(),
        P(("tx", "ty"), None),
        P(("tx", "ty"), None),
    )
    out_specs = P(("tx", "ty"), None, None)
    return jax.shard_map(shards, mesh=mesh, in_specs=in_specs, out_specs=out_specs, check_vma=False)
```

profile of v0, /device:TPU:1, one launch (start us, length us, event | category | flops | bytes accessed | tf_op | source)
XLA Modules:
  0.0 584.2 jit_solution(239053687158014245)
XLA Ops:
  0.0 1.7 convert_element_type.66
  1.7 4.6 collective-permute-start.2
  6.3 1.3 collective-permute-start.3
  7.6 4.1 collective-permute-start
  11.6 1.3 collective-permute-start.1
  12.9 0.7 broadcast_add_fusion
  13.6 0.7 broadcast_compare_fusion
  14.3 0.7 compare_select_fusion
  15.0 0.7 or_bitcast_fusion
  15.8 63.4 %gather_fusion.4 = f32[8192]{0:T(1024)S(1)} fusion(f32[4,8,2048]{2,1,0:T(8,128)S(1)} %copy-done.1, s32[8192]{0:T(1024)S(1)} %bitcast.229), kind=kCustom, calls=%fused_computation.4 | custom fusion | bytes 163840 | tf_op jit(solution)/shard_map/jit(take_along_axis)/gather | solution.py:64
  79.5 0.7 gather_fusion.1
  80.4 23.5 %all_gather.13 = f32[16,8,256]{2,1,0:T(8,128)S(1)} all-gather(f32[1,8,256]{2,1,0:T(8,128)S(1)} %copy.26), channel_id=1, replica_groups=mesh['tx'=8,'ty'=16] {'ty'}, dimensions={0}, use_global_device_ids=true | all-gather | bytes 139264 | tf_op jit(solution)/shard_map/all_gather | solution.py:69
  104.0 2.0 copy.27
  105.9 2.3 gather_fusion.3
  109.0 1.2 fusion.71
  110.2 1.2 compare_and_fusion.2
  111.6 20.4 %all_gather.15 = f32[8,8,256]{2,1,0:T(8,128)S(1)} all-gather(f32[1,8,256]{2,1,0:T(8,128)S(1)} %copy.28), channel_id=1, replica_groups=mesh['tx'=8,'ty'=16] {'tx'}, dimensions={0}, use_global_device_ids=true | all-gather | bytes 73728 | tf_op jit(solution)/shard_map/all_gather | solution.py:75
  132.6 1.2 slice_reduce_fusion.7
  133.7 4.4 fusion.28
  138.1 16.5 %all-gather = bf16[1024,256]{1,0:T(8,128)(2,1)S(1)} all-gather(bf16[64,256]{1,0:T(8,128)(2,1)} %fusion.28), channel_id=2, replica_groups=mesh['tx'=8,'ty'=16] {'ty'}, dimensions={0}, use_global_device_ids=true | all-gather | bytes 557056 | tf_op jit(solution)/shard_map/all_gather | solution.py:68
  154.6 1.7 fusion.29
  156.3 58.5 %psum.7 = bf16[1,64,256]{2,1,0:T(8,128)(2,1)} all-reduce(bf16[1,64,256]{2,1,0:T(8,128)(2,1)} %fusion.29), channel_id=1, replica_groups=mesh['tx'=8,'ty'=16] {'ty'}, use_global_device_ids=true, to_apply=%region_0.0 | all-reduce | flops 16384 | bytes 65536 | tf_op jit(solution)/shard_map/psum | solution.py:70
  214.8 33.8 %all_gather.14 = bf16[8,64,256]{2,1,0:T(8,128)(2,1)} all-gather(bf16[1,64,256]{2,1,0:T(8,128)(2,1)} %psum.7), channel_id=1, replica_groups=mesh['tx'=8,'ty'=16] {'tx'}, dimensions={0}, use_global_device_ids=true | all-gather | bytes 294912 | tf_op jit(solution)/shard_map/all_gather | solution.py:74
  248.6 1.2 pad_clamp_fusion.2
  249.8 2.2 gather_fusion.2
  251.9 0.9 broadcast_select_fusion
  253.5 1.1 slice_reduce_fusion.15
  254.7 1.4 gather_fusion
  256.1 0.7 copy_bitcast_fusion.6
  256.8 0.7 copy_bitcast_fusion.4
  257.5 0.7 copy_bitcast_fusion.2
  258.2 0.7 copy_bitcast_fusion.14
  258.9 0.7 copy_bitcast_fusion.12
  259.6 0.7 copy_bitcast_fusion.10
  260.4 0.7 copy_bitcast_fusion.8
  261.1 3.7 convolution_bitcast_fusion
  265.0 3.4 fusion.22
  268.5 4.6 fusion.24
  273.1 2.0 maximum_convert_fusion
  275.1 2.9 pad_maximum_fusion
  278.0 303.2 %while.13 = (s32[]{:T(128)}, f32[4,64,2048]{2,1,0:T(8,128)}, pred[4,3]{1,0:T(4,128)(4,1)S(1)}, s32[4,3]{1,0:T(4,128)S(1)}, bf16[12,64,2048]{2,1,0:T(8,128)(2,1)}...) while((s32[]{:T(128)}, f32[4,64,2048]{2,1,0:T(8,128)}, ...), condition=%wide.region_3.4_spmd, body=%wide.region_2.3_spmd.sunk | while | flops 1951006720 | bytes 4327891 | solution.py:122
  278.3 0.7 fusion.99
  284.6 1.9 constant_dynamic-slice_fusion.40
  286.5 0.7 fusion.100
  287.2 21.9 %fusion.101 = f32[64,2048]{1,0:T(8,128)S(1)} fusion(f32[2048]{0:T(1024)S(1)} %bitcast.242, f32[2048]{0:T(1024)S(1)} %bitcast.281, f32[2048]{0:T(1024)S(1)} %bitcast.260, f32[2048]{0:T(1024)S(1)} %bitcast.274, f32[2048]{0:T(1024)S(1)} %bitcast.257, f32[2048]{0:T(1024)S(1)} %bitcast.275, f32[2048]{0:T(1024)S(1)} %bitcast.254, f32[2048]{0:T(1024)S(1)} %bitcast.276, ...), kind=kOutput, calls=%fused_computation.17.clone.1 | convolution fusion | flops 650248192 | bytes 918020 | tf_op jit(solution)/shard_map/while/body/eval_jaxpr/dot_general | solution.py:106
  309.0 21.9 %fusion.102 = f32[64,2048]{1,0:T(8,128)S(1)} fusion(f32[64,2048]{1,0:T(8,128)S(1)} %fusion.101, f32[2048]{0:T(1024)S(1)} %bitcast.273, f32[2048]{0:T(1024)S(1)} %bitcast.266, f32[2048]{0:T(1024)S(1)} %bitcast.267, f32[2048]{0:T(1024)S(1)} %bitcast.268, f32[2048]{0:T(1024)S(1)} %bitcast.269, f32[2048]{0:T(1024)S(1)} %bitcast.270, ...), kind=kOutput, calls=%fused_computation.16.clone.1 | convolution fusion | flops 650379264 | bytes 1442308 | tf_op jit(solution)/shard_map/while/body/eval_jaxpr/dot_general | solution.py:106
  331.0 22.4 %fusion.103 = f32[4,64,2048]{2,1,0:T(8,128)} fusion(f32[4,64,2048]{2,1,0:T(8,128)} %get-tuple-element.377, s32[]{:T(128)} %get-tuple-element.376, f32[64,2048]{1,0:T(8,128)S(1)} %fusion.102, f32[2048]{0:T(1024)S(1)} %bitcast.241, f32[2048]{0:T(1024)S(1)} %bitcast.235, f32[2048]{0:T(1024)S(1)} %bitcast.236, f32[2048]{0:T(1024)S(1)} %bitcast.237, ...), kind=kOutput, calls=%fused_computation.14.clone.1 | convolution fusion | flops 650379264 | bytes 1442820 | tf_op jit(solution)/shard_map/while/body/eval_jaxpr/dot_general | solution.py:106
  353.8 0.7 fusion.99
  360.1 2.1 constant_dynamic-slice_fusion.40
  362.2 0.7 fusion.100
  362.9 21.5 %fusion.101 = f32[64,2048]{1,0:T(8,128)S(1)} fusion(f32[2048]{0:T(1024)S(1)} %bitcast.242, f32[2048]{0:T(1024)S(1)} %bitcast.281, f32[2048]{0:T(1024)S(1)} %bitcast.260, f32[2048]{0:T(1024)S(1)} %bitcast.274, f32[2048]{0:T(1024)S(1)} %bitcast.257, f32[2048]{0:T(1024)S(1)} %bitcast.275, f32[2048]{0:T(1024)S(1)} %bitcast.254, f32[2048]{0:T(1024)S(1)} %bitcast.276, ...), kind=kOutput, calls=%fused_computation.17.clone.1 | convolution fusion | flops 650248192 | bytes 918020 | tf_op jit(solution)/shard_map/while/body/eval_jaxpr/dot_general | solution.py:106
  384.4 22.0 %fusion.102 = f32[64,2048]{1,0:T(8,128)S(1)} fusion(f32[64,2048]{1,0:T(8,128)S(1)} %fusion.101, f32[2048]{0:T(1024)S(1)} %bitcast.273, f32[2048]{0:T(1024)S(1)} %bitcast.266, f32[2048]{0:T(1024)S(1)} %bitcast.267, f32[2048]{0:T(1024)S(1)} %bitcast.268, f32[2048]{0:T(1024)S(1)} %bitcast.269, f32[2048]{0:T(1024)S(1)} %bitcast.270, ...), kind=kOutput, calls=%fused_computation.16.clone.1 | convolution fusion | flops 650379264 | bytes 1442308 | tf_op jit(solution)/shard_map/while/body/eval_jaxpr/dot_general | solution.py:106
  406.4 22.5 %fusion.103 = f32[4,64,2048]{2,1,0:T(8,128)} fusion(f32[4,64,2048]{2,1,0:T(8,128)} %get-tuple-element.377, s32[]{:T(128)} %get-tuple-element.376, f32[64,2048]{1,0:T(8,128)S(1)} %fusion.102, f32[2048]{0:T(1024)S(1)} %bitcast.241, f32[2048]{0:T(1024)S(1)} %bitcast.235, f32[2048]{0:T(1024)S(1)} %bitcast.236, f32[2048]{0:T(1024)S(1)} %bitcast.237, ...), kind=kOutput, calls=%fused_computation.14.clone.1 | convolution fusion | flops 650379264 | bytes 1442820 | tf_op jit(solution)/shard_map/while/body/eval_jaxpr/dot_general | solution.py:106
  435.6 2.1 constant_dynamic-slice_fusion.40
  437.7 0.7 fusion.100
  438.4 21.5 %fusion.101 = f32[64,2048]{1,0:T(8,128)S(1)} fusion(f32[2048]{0:T(1024)S(1)} %bitcast.242, f32[2048]{0:T(1024)S(1)} %bitcast.281, f32[2048]{0:T(1024)S(1)} %bitcast.260, f32[2048]{0:T(1024)S(1)} %bitcast.274, f32[2048]{0:T(1024)S(1)} %bitcast.257, f32[2048]{0:T(1024)S(1)} %bitcast.275, f32[2048]{0:T(1024)S(1)} %bitcast.254, f32[2048]{0:T(1024)S(1)} %bitcast.276, ...), kind=kOutput, calls=%fused_computation.17.clone.1 | convolution fusion | flops 650248192 | bytes 918020 | tf_op jit(solution)/shard_map/while/body/eval_jaxpr/dot_general | solution.py:106
  459.9 22.0 %fusion.102 = f32[64,2048]{1,0:T(8,128)S(1)} fusion(f32[64,2048]{1,0:T(8,128)S(1)} %fusion.101, f32[2048]{0:T(1024)S(1)} %bitcast.273, f32[2048]{0:T(1024)S(1)} %bitcast.266, f32[2048]{0:T(1024)S(1)} %bitcast.267, f32[2048]{0:T(1024)S(1)} %bitcast.268, f32[2048]{0:T(1024)S(1)} %bitcast.269, f32[2048]{0:T(1024)S(1)} %bitcast.270, ...), kind=kOutput, calls=%fused_computation.16.clone.1 | convolution fusion | flops 650379264 | bytes 1442308 | tf_op jit(solution)/shard_map/while/body/eval_jaxpr/dot_general | solution.py:106
  481.9 22.4 %fusion.103 = f32[4,64,2048]{2,1,0:T(8,128)} fusion(f32[4,64,2048]{2,1,0:T(8,128)} %get-tuple-element.377, s32[]{:T(128)} %get-tuple-element.376, f32[64,2048]{1,0:T(8,128)S(1)} %fusion.102, f32[2048]{0:T(1024)S(1)} %bitcast.241, f32[2048]{0:T(1024)S(1)} %bitcast.235, f32[2048]{0:T(1024)S(1)} %bitcast.236, f32[2048]{0:T(1024)S(1)} %bitcast.237, ...), kind=kOutput, calls=%fused_computation.14.clone.1 | convolution fusion | flops 650379264 | bytes 1442820 | tf_op jit(solution)/shard_map/while/body/eval_jaxpr/dot_general | solution.py:106
  511.1 2.1 constant_dynamic-slice_fusion.40
  513.2 0.7 fusion.100
  513.9 21.5 %fusion.101 = f32[64,2048]{1,0:T(8,128)S(1)} fusion(f32[2048]{0:T(1024)S(1)} %bitcast.242, f32[2048]{0:T(1024)S(1)} %bitcast.281, f32[2048]{0:T(1024)S(1)} %bitcast.260, f32[2048]{0:T(1024)S(1)} %bitcast.274, f32[2048]{0:T(1024)S(1)} %bitcast.257, f32[2048]{0:T(1024)S(1)} %bitcast.275, f32[2048]{0:T(1024)S(1)} %bitcast.254, f32[2048]{0:T(1024)S(1)} %bitcast.276, ...), kind=kOutput, calls=%fused_computation.17.clone.1 | convolution fusion | flops 650248192 | bytes 918020 | tf_op jit(solution)/shard_map/while/body/eval_jaxpr/dot_general | solution.py:106
  535.4 22.0 %fusion.102 = f32[64,2048]{1,0:T(8,128)S(1)} fusion(f32[64,2048]{1,0:T(8,128)S(1)} %fusion.101, f32[2048]{0:T(1024)S(1)} %bitcast.273, f32[2048]{0:T(1024)S(1)} %bitcast.266, f32[2048]{0:T(1024)S(1)} %bitcast.267, f32[2048]{0:T(1024)S(1)} %bitcast.268, f32[2048]{0:T(1024)S(1)} %bitcast.269, f32[2048]{0:T(1024)S(1)} %bitcast.270, ...), kind=kOutput, calls=%fused_computation.16.clone.1 | convolution fusion | flops 650379264 | bytes 1442308 | tf_op jit(solution)/shard_map/while/body/eval_jaxpr/dot_general | solution.py:106
  557.4 22.5 %fusion.103 = f32[4,64,2048]{2,1,0:T(8,128)} fusion(f32[4,64,2048]{2,1,0:T(8,128)} %get-tuple-element.377, s32[]{:T(128)} %get-tuple-element.376, f32[64,2048]{1,0:T(8,128)S(1)} %fusion.102, f32[2048]{0:T(1024)S(1)} %bitcast.241, f32[2048]{0:T(1024)S(1)} %bitcast.235, f32[2048]{0:T(1024)S(1)} %bitcast.236, f32[2048]{0:T(1024)S(1)} %bitcast.237, ...), kind=kOutput, calls=%fused_computation.14.clone.1 | convolution fusion | flops 650379264 | bytes 1442820 | tf_op jit(solution)/shard_map/while/body/eval_jaxpr/dot_general | solution.py:106
  581.2 2.8 add_convert_fusion
  (75 shorter events, 4.3 us)
Async XLA Ops:
  0.0 133.7 %copy-start = (bf16[4,256,256]{2,1,0:T(8,128)(2,1)S(1)}, bf16[4,256,256]{2,1,0:T(8,128)(2,1)}, u32[]{:S(2)}) copy-start(bf16[4,256,256]{2,1,0:T(8,128)(2,1)} %param.18) | copy-start | bytes 1572868
  0.0 15.8 %copy-start.1 = (f32[4,8,2048]{2,1,0:T(8,128)S(1)}, f32[4,8,2048]{2,1,0:T(8,128)}, u32[]{:S(2)}) copy-start(f32[4,8,2048]{2,1,0:T(8,128)} %param.14) | copy-start | bytes 786436
  1.7 271.4 %collective-permute-start.2 = (bf16[4,8,2048]{2,1,0:T(8,128)(2,1)}, bf16[4,8,2048]{2,1,0:T(8,128)(2,1)}, u32[]{:S(2)}, u32[]{:S(2)}) collective-permute-start(bf16[4,8,2048]{2,1,0:T(8,128)(2,1)} %convert_element_type.66), channel_id=1, source_target_pairs={{0,1},{1,2},{2,3},{3,4},{4,5},{5,6},{6,7},{7,8},{8,9},{9,10},{10,1... | collective-permute-start | bytes 393224 | tf_op jit(solution)/shard_map/ppermute | solution.py:17
  6.3 266.8 %collective-permute-start.3 = (bf16[4,8,2048]{2,1,0:T(8,128)(2,1)}, bf16[4,8,2048]{2,1,0:T(8,128)(2,1)}, u32[]{:S(2)}, u32[]{:S(2)}) collective-permute-start(bf16[4,8,2048]{2,1,0:T(8,128)(2,1)} %convert_element_type.66), channel_id=1, source_target_pairs={{1,0},{2,1},{3,2},{4,3},{5,4},{6,5},{7,6},{8,7},{9,8},{10,9},{11,1... | collective-permute-start | bytes 393224 | tf_op jit(solution)/shard_map/ppermute | solution.py:19
  7.6 267.5 %collective-permute-start = (bf16[4,64,2048]{2,1,0:T(8,128)(2,1)}, bf16[4,64,2048]{2,1,0:T(8,128)(2,1)S(1)}, u32[]{:S(2)}, u32[]{:S(2)}) collective-permute-start(bf16[4,64,2048]{2,1,0:T(8,128)(2,1)} %param.13), channel_id=1, source_target_pairs={{0,1},{1,2},{2,3},{3,4},{4,5},{5,6},{6,7},{7,8},{8,9},{9,10},{10,1... | collective-permute-start | bytes 3145736 | tf_op jit(solution)/shard_map/ppermute | solution.py:17
  11.6 263.5 %collective-permute-start.1 = (bf16[4,64,2048]{2,1,0:T(8,128)(2,1)}, bf16[4,64,2048]{2,1,0:T(8,128)(2,1)}, u32[]{:S(2)}, u32[]{:S(2)}) collective-permute-start(bf16[4,64,2048]{2,1,0:T(8,128)(2,1)} %param.13), channel_id=1, source_target_pairs={{1,0},{2,1},{3,2},{4,3},{5,4},{6,5},{7,6},{8,7},{9,8},{10,9},{11,1... | collective-permute-start | bytes 3145736 | tf_op jit(solution)/shard_map/ppermute | solution.py:19
  15.8 63.5 %copy-start.7 = (s32[4,256]{1,0:T(4,128)S(1)}, s32[4,256]{1,0:T(4,128)}, u32[]{:S(2)}) copy-start(s32[4,256]{1,0:T(4,128)} %param.17) | copy-start | bytes 12292
  15.8 63.7 %copy-start.9 = (s32[1,256]{1,0:T(1,128)S(1)}, s32[1,256]{1,0:T(1,128)}, u32[]{:S(2)}) copy-start(s32[1,256]{1,0:T(1,128)} %param.19) | copy-start | bytes 3076
  79.2 54.5 %copy-start.3 = (bf16[4,64,2048]{2,1,0:T(8,128)(2,1)S(1)}, bf16[4,64,2048]{2,1,0:T(8,128)(2,1)}, u32[]{:S(2)}) copy-start(bf16[4,64,2048]{2,1,0:T(8,128)(2,1)} %param.13) | copy-start | bytes 3145732
  104.0 6.2 %copy-start.4 = (f32[16,8,256]{2,1,0:T(8,128)}, f32[16,8,256]{2,1,0:T(8,128)S(1)}, u32[]{:S(2)}) copy-start(f32[16,8,256]{2,1,0:T(8,128)S(1)} %all_gather.13) | copy-start | bytes 393220
  261.1 3.8 copy-start.6
  261.1 3.8 copy-start.10
  261.1 3.8 copy-start.11
  261.1 3.8 copy-start.12
  261.1 3.8 copy-start.13
  261.1 3.8 copy-start.14
  261.1 3.8 copy-start.15
  261.1 3.8 copy-start.16
  261.1 3.8 copy-start.17
  261.1 3.8 copy-start.18
  264.9 3.4 copy-start.5
  264.9 3.6 copy-start.8
  278.0 303.2 %copy-start.2 = (f32[4,64,2048]{2,1,0:T(8,128)S(1)}, f32[4,64,2048]{2,1,0:T(8,128)}, u32[]{:S(2)}) copy-start(f32[4,64,2048]{2,1,0:T(8,128)} %fusion.24) | copy-start | bytes 6291460
where the time goes:
time: 595 us; the launch traced here: 584 us
  matrix products  282 us (47%)
  blocking collectives  153 us (26%)
  local copies, waits for them, and re-layouts  94.7 us (16%)
  loops' own time  25.4 us (4%)
  other arithmetic  17.6 us (3%)
  starting transfers between devices  11.2 us (2%)
    dot_general x12, matrix products, near_tile(): jnp.dot(source_probes, kernel_block(source_points, own_points), preferred...  264 us
    gather x2, local copies, waits for them, and re-layouts, shards(): box_points = jnp.take_along_axis(points, index_box, axis=2)  63.4 us
    psum x1, blocking collectives, shards(): group_weight = lax.psum(node_term.astype(jnp.bfloat16), 'ty')  58.5 us
    all_gather x1, blocking collectives, shards(): every_weight = lax.all_gather(group_weight[None], 'tx', axis=0, tiled=True)  33.8 us
    another operation x1, loops' own time, shards(): lax.fori_loop(0, boxes, near_box, jnp.zeros((boxes, probe_count, leaf_cou...  25.4 us
    all_gather x1, blocking collectives, shards(): ty_points = lax.all_gather(node_points[None], 'ty', axis=0, tiled=True)  23.5 us
    all_gather x1, blocking collectives, shards(): every_points = lax.all_gather(own_group[None], 'tx', axis=0, tiled=True)  20.4 us
    all_gather x1, blocking collectives, shards(): ty_weights = lax.all_gather(node_weight[None], 'ty', axis=0, tiled=True)  16.5 us
  transfers between devices with their start and end apart: 4, of which 0 were waited for; matrix products, arithmetic and copies ran while one was open for 19% of the time, Pallas kernels for 0%

commit v1 on v0

v1 whole, which is shorter than its diff:
```python
import functools
import math

import jax
import jax.numpy as jnp
from jax import lax
from jax.experimental import pallas as pl
from jax.experimental.pallas import tpu as pltpu
from jax.sharding import PartitionSpec as P

bf16 = jnp.bfloat16
f32 = jnp.float32
i32 = jnp.int32

INV_LENGTH = 4.0
LN2 = math.log(2.0)
SCALE = INV_LENGTH / LN2
VMEM = pl.BlockSpec(memory_space=pltpu.VMEM)
SMEM = pl.BlockSpec(memory_space=pltpu.SMEM)
TILE_ROWS = 512
TILE_COLS = 1024
FIRST_UNITS = 2
SECOND_UNITS = 5
SLOTS = 12


def params(mib=48):
    return pltpu.CompilerParams(vmem_limit_bytes=mib * 2**20)


def split_points(points):
    scaled = (points - 0.5) * SCALE
    high = scaled.astype(bf16)
    low = (scaled - high.astype(f32)).astype(bf16)
    return high, low


def norm_rows(pair, one_first):
    high = pair[:8]
    low = pair[8:]
    full = high + low
    norm = jnp.sum(full * full, axis=0, keepdims=True)
    first = norm.astype(bf16).astype(f32)
    rest = norm - first
    second = rest.astype(bf16).astype(f32)
    third = rest - second
    row = lax.broadcasted_iota(i32, high.shape, 0)
    base = 3 if one_first else 0
    ones = 0 if one_first else 3
    out = jnp.where((row >= ones) & (row < ones + 3), 1.0, 0.0)
    out = jnp.where(row == base, first, out)
    out = jnp.where(row == base + 1, second, out)
    return jnp.where(row == base + 2, third, out)


def source_features(pair):
    high = pair[:8] * -2.0
    low = pair[8:] * -2.0
    return jnp.concatenate([high, low, high, norm_rows(pair, False)], axis=0).T.astype(bf16)


def target_features(pair):
    high = pair[:8]
    return jnp.concatenate([high, high, pair[8:], norm_rows(pair, True)], axis=0).astype(bf16)


def entries(squared):
    squared = jnp.maximum(squared, 1e-12)
    scaled = squared * lax.rsqrt(squared)
    return (scaled * jnp.exp2(-scaled)).astype(bf16)


def dot(a, b):
    return jnp.dot(a, b, preferred_element_type=f32)


def dot_nt(a, b):
    return lax.dot_general(a, b, (((1,), (1,)), ((), ())), preferred_element_type=f32)


def pack_kernel(near_ref, base_ref, probes_ref, points_ref, out_ref, table_ref):
    b = pl.program_id(0)
    out_ref[0, :64, :] = probes_ref[0]
    high, low = split_points(points_ref[0])
    out_ref[0, 64:80, :] = jnp.concatenate([high.astype(f32), low.astype(f32)], axis=0).astype(bf16)

    @pl.when(b == 0)
    def _():
        boxes, width = near_ref.shape
        count = i32(0)
        last = [i32(0), i32(0), i32(0)]
        own_count = i32(0)
        for own in (True, False):
            for box in range(boxes):
                for entry in range(width):
                    named = near_ref[box, entry]
                    slot = jnp.clip(named - base_ref[0], 0, 3 * boxes - 1)
                    side = (slot >= boxes).astype(i32) + (slot >= 2 * boxes).astype(i32)
                    mine = side == 1
                    take = (named >= 0) & (mine if own else jnp.logical_not(mine))
                    last = [jnp.where(take & (side == k), slot - k * boxes, last[k]) for k in range(3)]

                    @pl.when(take)
                    def _(count=count, box=box, side=side, last=tuple(last)):
                        table_ref[0, count] = side
                        table_ref[1, count] = i32(box)
                        table_ref[2, count] = last[0]
                        table_ref[3, count] = last[1]
                        table_ref[4, count] = last[2]

                    count = count + take.astype(i32)
            if own:
                own_count = count
        table_ref[5, 0] = count
        table_ref[5, 1] = own_count


def pack(near_list, base, probes, points):
    boxes, count, leaf = probes.shape
    return pl.pallas_call(
        pack_kernel,
        grid=(boxes,),
        in_specs=[
            SMEM,
            SMEM,
            pl.BlockSpec((1, count, leaf), lambda b: (b, 0, 0)),
            pl.BlockSpec((1, 8, leaf), lambda b: (b, 0, 0)),
        ],
        out_specs=[pl.BlockSpec((1, count + 16, leaf), lambda b: (b, 0, 0)), SMEM],
        out_shape=[
            jax.ShapeDtypeStruct((boxes, count + 16, leaf), bf16),
            jax.ShapeDtypeStruct((6, SLOTS), i32),
        ],
        compiler_params=params(),
        name="pack",
    )(near_list, base, probes, points)


def one_hot(index_row, size, offset=0):
    rows = lax.broadcasted_iota(i32, (size, index_row.shape[1]), 0) + offset
    return jnp.where(rows == index_row, 1.0, 0.0).astype(bf16)


def up_kernel(packed_ref, up_ref, box_skel_ref, transfer_ref, node_skel_ref, node_transfer_ref, out_ref, acc, pool):
    b = pl.program_id(0)
    boxes = pl.num_programs(0)
    rank = up_ref.shape[1]
    leaf = up_ref.shape[2]

    @pl.when(b == 0)
    def _():
        acc[...] = jnp.zeros_like(acc)

    weights = dot_nt(packed_ref[0, :64, :], up_ref[0]).astype(bf16)
    acc[...] += dot(weights, transfer_ref[0])
    pool[b] = dot(packed_ref[0, 64:80, :], one_hot(box_skel_ref[0], leaf)).astype(bf16)

    @pl.when(b == boxes - 1)
    def _():
        node_weight = acc[...].astype(bf16)
        out_ref[0:64, :] = node_weight
        found = jnp.zeros((16, rank), f32)
        for k in range(pool.shape[0]):
            found = found + dot(pool[k], one_hot(node_skel_ref[...], rank, k * rank))
        out_ref[64:80, :] = found.astype(bf16)
        out_ref[80:144, :] = dot(node_weight, node_transfer_ref[0]).astype(bf16)


def up_pass(packed, up_basis, box_skeleton, box_transfer, node_skeleton, node_transfer):
    boxes, rows, leaf = packed.shape
    rank = up_basis.shape[1]
    return pl.pallas_call(
        up_kernel,
        grid=(boxes,),
        in_specs=[
            pl.BlockSpec((1, rows, leaf), lambda b: (b, 0, 0)),
            pl.BlockSpec((1, rank, leaf), lambda b: (b, 0, 0)),
            pl.BlockSpec((1, 1, rank), lambda b: (b, 0, 0)),
            pl.BlockSpec((1, rank, rank), lambda b: (b, 0, 0)),
            pl.BlockSpec((1, rank), lambda b: (0, 0)),
            pl.BlockSpec((1, rank, rank), lambda b: (0, 0, 0)),
        ],
        out_specs=pl.BlockSpec((144, rank), lambda b: (0, 0)),
        out_shape=jax.ShapeDtypeStruct((144, rank), bf16),
        scratch_shapes=[pltpu.VMEM((64, rank), f32), pltpu.VMEM((boxes, 16, rank), bf16)],
        compiler_params=params(),
        name="up_pass",
    )(packed, up_basis, box_skeleton[:, None, :], box_transfer, node_skeleton, node_transfer)


def near_body(bounds, table, sources, target_ref, acc_ref, held, left, right):
    i = pl.program_id(0) + bounds[0]

    @pl.when(i < bounds[1])
    def _():
        side = table[0, i]
        box = table[1, i]
        for k, ref in sources:

            @pl.when(side == k)
            def _(ref=ref):
                held[...] = ref[0, :64, :]
                left[...] = source_features(ref[0, 64:80, :].astype(f32))

        right[...] = target_features(target_ref[0].astype(f32))
        leaf = left.shape[0]

        def columns(j, carry):
            cols = pl.ds(pl.multiple_of(j * TILE_COLS, TILE_COLS), TILE_COLS)
            total = acc_ref[box, :, cols]
            for k in range(leaf // TILE_ROWS):
                rows = slice(k * TILE_ROWS, (k + 1) * TILE_ROWS)
                block = entries(dot(left[rows, :], right[:, cols]))
                total = total + dot(held[:, rows], block)
            acc_ref[box, :, cols] = total
            return carry

        lax.fori_loop(0, leaf // TILE_COLS, columns, 0)


def near_first_kernel(bounds, table, own_ref, target_ref, acc_ref, held, left, right):
    @pl.when(pl.program_id(0) == 0)
    def _():
        acc_ref[...] = jnp.zeros_like(acc_ref)

    near_body(bounds, table, [(1, own_ref)], target_ref, acc_ref, held, left, right)


def near_kernel(bounds, table, own_ref, target_ref, prev_ref, next_ref, in_ref, acc_ref, held, left, right):
    @pl.when(pl.program_id(0) == 0)
    def _():
        acc_ref[...] = in_ref[...]

    near_body(bounds, table, [(0, prev_ref), (1, own_ref), (2, next_ref)], target_ref, acc_ref, held, left, right)


def last_unit(i, bounds):
    return jnp.maximum(jnp.minimum(i + bounds[0], bounds[1] - 1), 0)


def near_part(steps, bounds, table, packed, halo=None, acc=None):
    boxes, rows, leaf = packed.shape

    def source(row):
        def index(i, bounds, table):
            return (table[row, last_unit(i, bounds)], 0, 0)

        return pl.BlockSpec((1, rows, leaf), index)

    def target(i, bounds, table):
        return (table[1, last_unit(i, bounds)], 4, 0)

    in_specs = [source(3), pl.BlockSpec((1, 16, leaf), target)]
    args = [packed, packed]
    if halo is not None:
        in_specs += [source(2), source(4), pl.BlockSpec((boxes, 64, leaf), lambda i, bounds, table: (0, 0, 0))]
        args += [halo[0], halo[1], acc]
    tile = leaf * leaf
    return pl.pallas_call(
        near_first_kernel if halo is None else near_kernel,
        grid_spec=pltpu.PrefetchScalarGridSpec(
            num_scalar_prefetch=2,
            grid=(steps,),
            in_specs=in_specs,
            out_specs=pl.BlockSpec((boxes, 64, leaf), lambda i, bounds, table: (0, 0, 0)),
            scratch_shapes=[
                pltpu.VMEM((64, leaf), bf16),
                pltpu.VMEM((leaf, 32), bf16),
                pltpu.VMEM((32, leaf), bf16),
            ],
        ),
        out_shape=jax.ShapeDtypeStruct((boxes, 64, leaf), f32),
        compiler_params=params(),
        cost_estimate=pl.CostEstimate(
            flops=3 * 2 * tile * 320, bytes_accessed=8 * 2**20, transcendentals=3 * 2 * tile
        ),
        name="near_part",
    )(bounds, table, *args)


def fold_kernel(*refs):
    out_ref = refs[-1]
    total = jnp.zeros((64, out_ref.shape[1]), f32)
    for k, ref in enumerate(refs[:-1]):
        out_ref[k * 80 : (k + 1) * 80, :] = ref[0:80, :]
        total = total + ref[80:144, :].astype(f32)
    out_ref[320:384, :] = total.astype(bf16)


def fold(parts):
    rank = parts[0].shape[1]
    return pl.pallas_call(
        fold_kernel,
        in_specs=[VMEM] * len(parts),
        out_specs=VMEM,
        out_shape=jax.ShapeDtypeStruct((384, rank), bf16),
        compiler_params=params(),
        name="fold",
    )(*parts)


def group_kernel(order_ref, skel_ref, *refs):
    out_ref = refs[-1]
    parts = refs[:-1]
    rank = out_ref.shape[1]
    total = jnp.zeros((64, rank), f32)
    found = jnp.zeros((16, rank), f32)
    skeleton = skel_ref[0]
    for z, ref in enumerate(parts):
        total = total + ref[320:384, :].astype(f32)
        for x in range(4):
            hot = one_hot(skeleton, rank, order_ref[z * 4 + x] * rank)
            found = found + dot(ref[x * 80 + 64 : x * 80 + 80, :], hot)
    out_ref[0:64, :] = total.astype(bf16)
    out_ref[64:80, :] = found.astype(bf16)


def group_pass(order, group_skeleton, tx_index, parts):
    rank = parts[0].shape[1]
    own = lax.dynamic_slice_in_dim(group_skeleton, tx_index, 1, 0)[None]
    return pl.pallas_call(
        group_kernel,
        in_specs=[SMEM] + [VMEM] * 5,
        out_specs=VMEM,
        out_shape=jax.ShapeDtypeStruct((80, rank), bf16),
        compiler_params=params(),
        name="group_pass",
    )(order, own, *parts)


def far_kernel(slot_ref, own_ref, p0, p1, p2, p3, out_ref, pool):
    for z, ref in enumerate((p0, p1, p2, p3)):
        for x in range(4):
            pool[z * 4 + x] = ref[x * 80 : (x + 1) * 80, :]
    target = target_features(own_ref[64:80, :].astype(f32))
    total = jnp.zeros(out_ref.shape, f32)
    for k in range(slot_ref.shape[0]):
        slot = slot_ref[k]
        left = source_features(pool[slot, 64:80, :].astype(f32))
        total = total + dot(pool[slot, 0:64, :], entries(dot(left, target)))
    out_ref[...] = total * LN2


def far_pass(slots, own, parts):
    rank = own.shape[1]
    return pl.pallas_call(
        far_kernel,
        in_specs=[SMEM] + [VMEM] * 5,
        out_specs=VMEM,
        out_shape=jax.ShapeDtypeStruct((64, rank), f32),
        scratch_shapes=[pltpu.VMEM((16, 80, rank), bf16)],
        compiler_params=params(),
        name="far_pass",
    )(slots, own, *parts)


def down_kernel(far_ref, node_transfer_ref, transfer_ref, down_ref, near_ref, own_ref, *refs):
    out_ref, potential = refs[-2:]
    others = refs[:-2]

    @pl.when(pl.program_id(0) == 0)
    def _():
        target = target_features(own_ref[64:80, :].astype(f32))
        total = jnp.zeros(far_ref.shape, f32)
        for ref in others:
            left = source_features(ref[64:80, :].astype(f32))
            total = total + dot(ref[0:64, :], entries(dot(left, target)))
        group_potential = (total * LN2).astype(bf16)
        pushed = dot_nt(group_potential, node_transfer_ref[0])
        potential[...] = (far_ref[...] + pushed).astype(bf16)

    box_potential = dot_nt(potential[...], transfer_ref[0]).astype(bf16)
    out_ref[0] = (dot(box_potential, down_ref[0]) + near_ref[0] * LN2).astype(bf16)


def down_pass(far, node_transfer, box_transfer, down_basis, near, own, others):
    boxes, rank, leaf = down_basis.shape

    def whole(shape):
        return pl.BlockSpec(shape, lambda b: (0,) * len(shape))

    return pl.pallas_call(
        down_kernel,
        grid=(boxes,),
        in_specs=[
            whole((64, rank)),
            whole((1, rank, rank)),
            pl.BlockSpec((1, rank, rank), lambda b: (b, 0, 0)),
            pl.BlockSpec((1, rank, leaf), lambda b: (b, 0, 0)),
            pl.BlockSpec((1, 64, leaf), lambda b: (b, 0, 0)),
        ]
        + [whole((80, rank))] * (1 + len(others)),
        out_specs=pl.BlockSpec((1, 64, leaf), lambda b: (b, 0, 0)),
        out_shape=jax.ShapeDtypeStruct((boxes, 64, leaf), bf16),
        scratch_shapes=[pltpu.VMEM((64, rank), bf16)],
        compiler_params=params(),
        name="down_pass",
    )(far, node_transfer, box_transfer, down_basis, near, own, *others)


def shards(
    probes,
    points,
    up_basis,
    down_basis,
    box_skeleton,
    box_transfer,
    node_skeleton,
    node_transfer,
    group_skeleton,
    near_list,
    node_list,
):
    boxes = probes.shape[0]
    n_tx = lax.axis_size("tx")
    n_ty = lax.axis_size("ty")
    tx_index = lax.axis_index("tx")
    ty_index = lax.axis_index("ty")
    node = tx_index * n_ty + ty_index
    z_index, x_index = ty_index // 4, ty_index % 4
    base = ((node - 1) * boxes).astype(i32).reshape(1)

    packed, table = pack(near_list, base, probes, points)
    prev_box = lax.ppermute(packed, "ty", [(i, i + 1) for i in range(n_ty - 1)])
    next_box = lax.ppermute(packed, "ty", [(i + 1, i) for i in range(n_ty - 1)])
    count = table[5, 0]
    cut_one = jnp.minimum(table[5, 1], FIRST_UNITS)
    cut_two = jnp.minimum(count, SECOND_UNITS)

    own = up_pass(packed, up_basis, box_skeleton, box_transfer, node_skeleton, node_transfer)
    row = [own] + [
        lax.ppermute(own, "ty", [(i, (i // 4) * 4 + (i + s) % 4) for i in range(n_ty)]) for s in (1, 2, 3)
    ]
    near = near_part(FIRST_UNITS, jnp.stack([jnp.zeros_like(cut_one), cut_one]), table, packed)
    near, row = lax.optimization_barrier((near, row))

    folded = fold(row)
    parts = [folded] + [
        lax.ppermute(folded, "ty", [(i, (i + 4 * s) % n_ty) for i in range(n_ty)]) for s in (1, 2, 3)
    ]
    near = near_part(SECOND_UNITS, jnp.stack([cut_one, cut_two]), table, packed, (prev_box, next_box), near)
    near, parts = lax.optimization_barrier((near, parts))

    slots = jnp.arange(n_ty, dtype=i32)
    order = ((z_index - slots // 4) % 4) * 4 + (x_index - slots % 4) % 4
    group = group_pass(order.astype(i32), group_skeleton, tx_index, parts)
    others = [lax.ppermute(group, "tx", [(i, (i + s) % n_tx) for i in range(n_tx)]) for s in range(1, n_tx)]
    named = node_list[0] - tx_index * n_ty
    far_slots = ((z_index - named // 4) % 4) * 4 + (x_index - named % 4) % 4
    far = far_pass(far_slots.astype(i32), own, parts)
    near = near_part(SLOTS - SECOND_UNITS, jnp.stack([cut_two, count]), table, packed, (prev_box, next_box), near)
    near, others, far = lax.optimization_barrier((near, others, far))
    return down_pass(far, node_transfer, box_transfer, down_basis, near, group, others)


def solution(mesh):
    spec3 = P(("tx", "ty"), None, None)
    spec2 = P(("tx", "ty"), None)
    in_specs = (spec3, spec3, spec3, spec3, spec2, spec3, spec2, spec3, P(), spec2, spec2)
    return jax.shard_map(shards, mesh=mesh, in_specs=in_specs, out_specs=spec3, check_vma=False)
```

time: 595 us -> 152 us (0.26)
  the two profiles are of different devices: /device:TPU:1 before, /device:TPU:95 now
where the time goes in v1:
time: 152 us; the launch traced here: 154 us
  Pallas kernels  101 us (66%)
  starting transfers between devices  34.5 us (23%)
  local copies, waits for them, and re-layouts  9.45 us (6%)
  waiting for transfers between devices  7.27 us (5%)
    pallas_call x3, Pallas kernels, near_part(): pl.pallas_call(near_first_kernel if halo is None else near_kernel, grid_s...  84.7 us
    ppermute x7, starting transfers between devices, shards(): lax.ppermute(group, 'tx', [(i, (i + s) % n_tx) for i in range(n_tx)])  22 us
    unnamed x24, local copies, waits for them, and re-layouts  8.16 us
    ppermute x1, waiting for transfers between devices, shards(): next_box = lax.ppermute(packed, 'ty', [(i + 1, i) for i in range(n_ty - 1)])  6.34 us
    pallas_call x1, Pallas kernels, down_pass(): pl.pallas_call(down_kernel, grid=(boxes,), in_specs=[whole((64, rank)), w...  6.04 us
    pallas_call x1, Pallas kernels, up_pass(): pl.pallas_call(up_kernel, grid=(boxes,), in_specs=[pl.BlockSpec((1, rows,...  5.55 us
    ppermute x1, starting transfers between devices, shards(): prev_box = lax.ppermute(packed, 'ty', [(i, i + 1) for i in range(n_ty - 1)])  5.42 us
    ppermute x3, starting transfers between devices, shards(): lax.ppermute(own, 'ty', [(i, i // 4 * 4 + (i + s) % 4) for i in range(n_t...  3.26 us
  transfers between devices with their start and end apart: 15, of which 2 were waited for; matrix products, arithmetic and copies ran while one was open for 1% of the time, Pallas kernels for 56%

profile of v1, /device:TPU:95, one launch (start us, length us, event | category | flops | bytes accessed | tf_op | source)
XLA Modules:
  0.0 154.2 jit_solution(6841726418902819048)
XLA Ops:
  0.0 0.0 copy-start
  0.0 0.7 broadcast_in_dim.6.box_skel_ref
  0.7 0.0 copy-start.3
  0.7 1.2 copy-done.3
  1.9 0.0 copy-start.6
  1.9 0.9 copy-done.6
  2.9 0.0 copy-start.7
  2.9 0.7 copy-done.7
  3.6 1.8 %pack.1 = (bf16[4,80,2048]{2,1,0:T(8,128)(2,1)S(1)}, s32[6,12]{1,0:T(8,128)S(1)}) custom-call(s32[4,3]{1,0:T(4,128)S(1)} %copy-done.7, s32[1]{0:T(128)} %bitcast.base_ref, bf16[4,64,2048]{2,1,0:T(8,128)(2,1)S(1)} %copy-done.3, f32[4,8,2048]{2,1,0:T(8,128)S(1)} %copy-done.6), custom_call_target="tpu_custom_call" | custom-call | tf_op jit(solution)/shard_map/pack/pallas_call | solution.py:120
  5.3 0.0 copy-start.1
  5.3 1.0 copy-done.1
  6.4 0.0 copy-start.4
  6.4 0.9 copy-done.4
  7.3 0.7 copy-done.8
  8.0 0.0 copy-start.11
  8.0 5.5 %up_pass.1.refs_0_.own_ref = bf16[144,256]{1,0:T(8,128)(2,1)S(1)} custom-call(bf16[4,80,2048]{2,1,0:T(8,128)(2,1)S(1)} %get-tuple-element.27.own_ref.target_ref.packed_ref, bf16[4,256,2048]{2,1,0:T(8,128)(2,1)} %up_ref.1, s32[4,1,256]{2,1,0:T(1,128)S(1)} %broadcast_in_dim.6.box_skel_ref, bf16[4,256,256]{2,1,0:T(8,128)(2,1)S(1)} %copy-done.1, ...), custom_call_target="tpu_custom_call" | custom-call | tf_op jit(solution)/shard_map/up_pass/pallas_call | solution.py:172
  13.5 0.6 collective-permute-start.4
  14.1 0.8 collective-permute-start.3
  15.0 1.8 %collective-permute-start.2 = (bf16[144,256]{1,0:T(8,128)(2,1)S(1)}, bf16[144,256]{1,0:T(8,128)(2,1)S(1)}, u32[]{:S(2)}, u32[]{:S(2)}) collective-permute-start(bf16[144,256]{1,0:T(8,128)(2,1)S(1)} %up_pass.1.refs_0_.own_ref), channel_id=1, source_target_pairs={{0,1},{1,2},{2,3},{3,0},{4,5},{5,6},{6,7},{7,4},{8,9},{9,10},{10,1... | collective-permute-start | bytes 221192 | tf_op jit(solution)/shard_map/ppermute | solution.py:432
  16.8 2.0 %collective-permute-start.1 = (bf16[4,80,2048]{2,1,0:T(8,128)(2,1)S(1)}, bf16[4,80,2048]{2,1,0:T(8,128)(2,1)S(1)}, u32[]{:S(2)}, u32[]{:S(2)}) collective-permute-start(bf16[4,80,2048]{2,1,0:T(8,128)(2,1)S(1)} %get-tuple-element.27.own_ref.target_ref.packed_ref), channel_id=1, source_target_pairs={{1,0},{2,1},{3,2},{4,3},{5,4},{6,5},{7,6},{8,7},{9,8},{10,9},{11,1... | collective-permute-start | bytes 3932168 | tf_op jit(solution)/shard_map/ppermute | solution.py:425
  18.8 5.4 %collective-permute-start = (bf16[4,80,2048]{2,1,0:T(8,128)(2,1)S(1)}, bf16[4,80,2048]{2,1,0:T(8,128)(2,1)}, u32[]{:S(2)}, u32[]{:S(2)}) collective-permute-start(bf16[4,80,2048]{2,1,0:T(8,128)(2,1)S(1)} %get-tuple-element.27.own_ref.target_ref.packed_ref), channel_id=1, source_target_pairs={{0,1},{1,2},{2,3},{3,4},{4,5},{5,6},{6,7},{7,8},{8,9},{9,10},{10,1... | collective-permute-start | bytes 3932168 | tf_op jit(solution)/shard_map/ppermute | solution.py:424
  24.2 0.6 fusion.11
  26.0 0.1 pad_add_fusion.2.bounds
  26.1 0.0 copy-done
  26.1 0.0 copy-done.11
  26.1 13.8 %near_part.3.in_ref = f32[4,64,2048]{2,1,0:T(8,128)S(1)} custom-call(s32[2]{0:T(128)S(1)} %pad_add_fusion.2.bounds, s32[6,12]{1,0:T(8,128)S(1)} %get-tuple-element.26.table, bf16[4,80,2048]{2,1,0:T(8,128)(2,1)S(1)} %get-tuple-element.27.own_ref.target_ref.packed_ref, bf16[4,80,2048]{2,1,0:T(8,128)(2,1)S(1)} %get-tuple-element.27.own_ref.target_ref.packed_ref), custom_call_target="tpu_custom_call" | custom-call | flops 8053063680 | bytes 8388608 | tf_op jit(solution)/shard_map/near_part/pallas_call | solution.py:259
  40.0 0.0 copy-start.10
  40.0 1.3 copy-done.10
  41.3 0.1 pad_add_fusion.1.bounds
  41.4 0.0 collective-permute-done.4.refs_3_
  41.4 0.0 collective-permute-done.3.refs_2_
  41.4 0.0 collective-permute-done.2.refs_1_
  41.4 0.1 collective-permute-start.7
  41.5 0.1 collective-permute-start.6
  41.6 1.6 %collective-permute-start.5 = (bf16[384,256]{1,0:T(8,128)(2,1)S(1)}, bf16[384,256]{1,0:T(8,128)(2,1)S(1)}, u32[]{:S(2)}, u32[]{:S(2)}) collective-permute-start(bf16[384,256]{1,0:T(8,128)(2,1)S(1)} %fold.1.refs_0_.p0), channel_id=1, source_target_pairs={{0,4},{1,5},{2,6},{3,7},{4,8},{5,9},{6,10},{7,11},{8,12},{9,13},{1... | collective-permute-start | bytes 589832 | tf_op jit(solution)/shard_map/ppermute | solution.py:439
  43.2 6.3 %collective-permute-done.1.next_ref = bf16[4,80,2048]{2,1,0:T(8,128)(2,1)S(1)} collective-permute-done((bf16[4,80,2048]{2,1,0:T(8,128)(2,1)S(1)}, bf16[4,80,2048]{2,1,0:T(8,128)(2,1)S(1)}, u32[]{:S(2)}, u32[]{:S(2)}) %collective-permute-start.1) | collective-permute-done | bytes 1310752 | tf_op jit(solution)/shard_map/ppermute | solution.py:425
  49.6 0.9 collective-permute-done.prev_ref
  50.5 22.3 %near_part.4.in_ref = f32[4,64,2048]{2,1,0:T(8,128)S(1)} custom-call(s32[2]{0:T(128)S(1)} %pad_add_fusion.1.bounds, s32[6,12]{1,0:T(8,128)S(1)} %get-tuple-element.26.table, bf16[4,80,2048]{2,1,0:T(8,128)(2,1)S(1)} %get-tuple-element.27.own_ref.target_ref.packed_ref, bf16[4,80,2048]{2,1,0:T(8,128)(2,1)S(1)} %get-tuple-element.27.own_ref.target_ref.packed_ref, ...), custom_call_target="tpu_custom_call" | custom-call | flops 8053063680 | bytes 8388608 | tf_op jit(solution)/shard_map/near_part/pallas_call | solution.py:259
  72.8 0.0 copy-start.9
  72.8 1.3 copy-done.9
  74.1 0.0 collective-permute-done.7.refs_3_.p3
  74.1 0.0 collective-permute-done.6.refs_2_.p2
  74.1 0.0 collective-permute-done.5.refs_1_.p1
  74.1 0.9 group_pass.1.own_ref
  75.1 15.8 %collective-permute-start.14 = (bf16[80,256]{1,0:T(8,128)(2,1)S(1)}, bf16[80,256]{1,0:T(8,128)(2,1)S(1)}, u32[]{:S(2)}, u32[]{:S(2)}) collective-permute-start(bf16[80,256]{1,0:T(8,128)(2,1)S(1)} %group_pass.1.own_ref), channel_id=1, source_target_pairs={{0,112},{16,0},{32,16},{48,32},{64,48},{80,64},{96,80},{112,96},{1... | collective-permute-start | bytes 122888 | tf_op jit(solution)/shard_map/ppermute | solution.py:447
  90.8 0.0 collective-permute-start.13
  90.9 0.6 pad_add_fusion.bounds
  91.5 0.0 collective-permute-start.12
  91.5 4.0 %collective-permute-start.11 = (bf16[80,256]{1,0:T(8,128)(2,1)S(1)}, bf16[80,256]{1,0:T(8,128)(2,1)S(1)}, u32[]{:S(2)}, u32[]{:S(2)}) collective-permute-start(bf16[80,256]{1,0:T(8,128)(2,1)S(1)} %group_pass.1.own_ref), channel_id=1, source_target_pairs={{0,64},{16,80},{32,96},{48,112},{64,0},{80,16},{96,32},{112,48},{1... | collective-permute-start | bytes 122888 | tf_op jit(solution)/shard_map/ppermute | solution.py:447
  95.5 0.0 collective-permute-start.10
  95.5 0.0 collective-permute-done.14.refs_6_
  95.5 2.2 %collective-permute-start.9 = (bf16[80,256]{1,0:T(8,128)(2,1)S(1)}, bf16[80,256]{1,0:T(8,128)(2,1)S(1)}, u32[]{:S(2)}, u32[]{:S(2)}) collective-permute-start(bf16[80,256]{1,0:T(8,128)(2,1)S(1)} %group_pass.1.own_ref), channel_id=1, source_target_pairs={{0,32},{16,48},{32,64},{48,80},{64,96},{80,112},{96,0},{112,16},{1... | collective-permute-start | bytes 122888 | tf_op jit(solution)/shard_map/ppermute | solution.py:447
  97.7 0.0 collective-permute-done.13.refs_5_
  97.7 0.1 collective-permute-start.8
  97.8 48.5 %near_part.5.near_ref = f32[4,64,2048]{2,1,0:T(8,128)S(1)} custom-call(s32[2]{0:T(128)S(1)} %pad_add_fusion.bounds, s32[6,12]{1,0:T(8,128)S(1)} %get-tuple-element.26.table, bf16[4,80,2048]{2,1,0:T(8,128)(2,1)S(1)} %get-tuple-element.27.own_ref.target_ref.packed_ref, bf16[4,80,2048]{2,1,0:T(8,128)(2,1)S(1)} %get-tuple-element.27.own_ref.target_ref.packed_ref, ...), custom_call_target="tpu_custom_call" | custom-call | flops 8053063680 | bytes 8388608 | tf_op jit(solution)/shard_map/near_part/pallas_call | solution.py:259
  146.3 1.8 %far_pass.1.far_ref = f32[64,256]{1,0:T(8,128)S(1)} custom-call(s32[8]{0:T(128)S(1)} %fusion.2.slot_ref, bf16[144,256]{1,0:T(8,128)(2,1)S(1)} %up_pass.1.refs_0_.own_ref, bf16[384,256]{1,0:T(8,128)(2,1)S(1)} %fold.1.refs_0_.p0, bf16[384,256]{1,0:T(8,128)(2,1)S(1)} %collective-permute-done.5.refs_1_.p1, ...), custom_call_target="tpu_custom_call" | custom-call | tf_op jit(solution)/shard_map/far_pass/pallas_call | solution.py:346
  148.1 0.0 collective-permute-done.12.refs_4_
  148.1 0.0 collective-permute-done.11.refs_3_
  148.1 0.0 collective-permute-done.10.refs_2_
  148.2 0.0 collective-permute-done.9.refs_1_
  148.2 0.0 collective-permute-done.8.refs_0_
  148.2 0.0 copy-done.2
  148.2 0.0 copy-done.5
  148.2 6.0 %down_pass.1 = bf16[4,64,2048]{2,1,0:T(8,128)(2,1)} custom-call(f32[64,256]{1,0:T(8,128)S(1)} %far_pass.1.far_ref, bf16[1,256,256]{2,1,0:T(8,128)(2,1)S(1)} %copy-done.5, bf16[4,256,256]{2,1,0:T(8,128)(2,1)S(1)} %copy-done.2, bf16[4,256,2048]{2,1,0:T(8,128)(2,1)} %down_ref.1, f32[4,64,2048]{2,1,0:T(8,128)S(1)} %near_part.5.near_ref, ...), custom_call_target="tpu_custom_call" | custom-call | tf_op jit(solution)/shard_map/down_pass/pallas_call | solution.py:382
  (7 shorter events, 0.1 us)
Async XLA Ops:
  0.0 26.1 %copy-start = (s32[8,256]{1,0:T(8,128)S(1)}, s32[8,256]{1,0:T(8,128)}, u32[]{:S(2)}) copy-start(s32[8,256]{1,0:T(8,128)} %param.19) | copy-start | bytes 24580
  0.7 1.2 copy-start.3
  1.9 0.9 copy-start.6
  2.9 0.7 copy-start.7
  5.3 1.0 copy-start.1
  6.4 0.9 copy-start.4
  7.3 0.7 copy-start.8
  8.0 18.1 %copy-start.11 = (s32[1,8]{1,0:T(1,128)S(1)}, s32[1,8]{1,0:T(1,128)}, u32[]{:S(2)}) copy-start(s32[1,8]{1,0:T(1,128)} %param.21) | copy-start | bytes 100
  13.5 27.9 %collective-permute-start.4 = (bf16[144,256]{1,0:T(8,128)(2,1)S(1)}, bf16[144,256]{1,0:T(8,128)(2,1)S(1)}, u32[]{:S(2)}, u32[]{:S(2)}) collective-permute-start(bf16[144,256]{1,0:T(8,128)(2,1)S(1)} %up_pass.1.refs_0_.own_ref), channel_id=1, source_target_pairs={{0,3},{1,0},{2,1},{3,2},{4,7},{5,4},{6,5},{7,6},{8,11},{9,8},{10,9... | collective-permute-start | bytes 221192 | tf_op jit(solution)/shard_map/ppermute | solution.py:432
  14.1 27.3 %collective-permute-start.3 = (bf16[144,256]{1,0:T(8,128)(2,1)S(1)}, bf16[144,256]{1,0:T(8,128)(2,1)S(1)}, u32[]{:S(2)}, u32[]{:S(2)}) collective-permute-start(bf16[144,256]{1,0:T(8,128)(2,1)S(1)} %up_pass.1.refs_0_.own_ref), channel_id=1, source_target_pairs={{0,2},{1,3},{2,0},{3,1},{4,6},{5,7},{6,4},{7,5},{8,10},{9,11},{10,... | collective-permute-start | bytes 221192 | tf_op jit(solution)/shard_map/ppermute | solution.py:432
  15.0 26.4 %collective-permute-start.2 = (bf16[144,256]{1,0:T(8,128)(2,1)S(1)}, bf16[144,256]{1,0:T(8,128)(2,1)S(1)}, u32[]{:S(2)}, u32[]{:S(2)}) collective-permute-start(bf16[144,256]{1,0:T(8,128)(2,1)S(1)} %up_pass.1.refs_0_.own_ref), channel_id=1, source_target_pairs={{0,1},{1,2},{2,3},{3,0},{4,5},{5,6},{6,7},{7,4},{8,9},{9,10},{10,1... | collective-permute-start | bytes 221192 | tf_op jit(solution)/shard_map/ppermute | solution.py:432
  16.8 32.8 %collective-permute-start.1 = (bf16[4,80,2048]{2,1,0:T(8,128)(2,1)S(1)}, bf16[4,80,2048]{2,1,0:T(8,128)(2,1)S(1)}, u32[]{:S(2)}, u32[]{:S(2)}) collective-permute-start(bf16[4,80,2048]{2,1,0:T(8,128)(2,1)S(1)} %get-tuple-element.27.own_ref.target_ref.packed_ref), channel_id=1, source_target_pairs={{1,0},{2,1},{3,2},{4,3},{5,4},{6,5},{7,6},{8,7},{9,8},{10,9},{11,1... | collective-permute-start | bytes 3932168 | tf_op jit(solution)/shard_map/ppermute | solution.py:425
  18.8 31.7 %collective-permute-start = (bf16[4,80,2048]{2,1,0:T(8,128)(2,1)S(1)}, bf16[4,80,2048]{2,1,0:T(8,128)(2,1)}, u32[]{:S(2)}, u32[]{:S(2)}) collective-permute-start(bf16[4,80,2048]{2,1,0:T(8,128)(2,1)S(1)} %get-tuple-element.27.own_ref.target_ref.packed_ref), channel_id=1, source_target_pairs={{0,1},{1,2},{2,3},{3,4},{4,5},{5,6},{6,7},{7,8},{8,9},{9,10},{10,1... | collective-permute-start | bytes 3932168 | tf_op jit(solution)/shard_map/ppermute | solution.py:424
  40.0 1.3 copy-start.10
  41.4 32.7 %collective-permute-start.7 = (bf16[384,256]{1,0:T(8,128)(2,1)S(1)}, bf16[384,256]{1,0:T(8,128)(2,1)S(1)}, u32[]{:S(2)}, u32[]{:S(2)}) collective-permute-start(bf16[384,256]{1,0:T(8,128)(2,1)S(1)} %fold.1.refs_0_.p0), channel_id=1, source_target_pairs={{0,12},{1,13},{2,14},{3,15},{4,0},{5,1},{6,2},{7,3},{8,4},{9,5},{1... | collective-permute-start | bytes 589832 | tf_op jit(solution)/shard_map/ppermute | solution.py:439
  41.5 32.6 %collective-permute-start.6 = (bf16[384,256]{1,0:T(8,128)(2,1)S(1)}, bf16[384,256]{1,0:T(8,128)(2,1)S(1)}, u32[]{:S(2)}, u32[]{:S(2)}) collective-permute-start(bf16[384,256]{1,0:T(8,128)(2,1)S(1)} %fold.1.refs_0_.p0), channel_id=1, source_target_pairs={{0,8},{1,9},{2,10},{3,11},{4,12},{5,13},{6,14},{7,15},{8,0},{9,1},... | collective-permute-start | bytes 589832 | tf_op jit(solution)/shard_map/ppermute | solution.py:439
  41.6 32.5 %collective-permute-start.5 = (bf16[384,256]{1,0:T(8,128)(2,1)S(1)}, bf16[384,256]{1,0:T(8,128)(2,1)S(1)}, u32[]{:S(2)}, u32[]{:S(2)}) collective-permute-start(bf16[384,256]{1,0:T(8,128)(2,1)S(1)} %fold.1.refs_0_.p0), channel_id=1, source_target_pairs={{0,4},{1,5},{2,6},{3,7},{4,8},{5,9},{6,10},{7,11},{8,12},{9,13},{1... | collective-permute-start | bytes 589832 | tf_op jit(solution)/shard_map/ppermute | solution.py:439
  72.8 1.3 copy-start.9
  75.1 20.5 %collective-permute-start.14 = (bf16[80,256]{1,0:T(8,128)(2,1)S(1)}, bf16[80,256]{1,0:T(8,128)(2,1)S(1)}, u32[]{:S(2)}, u32[]{:S(2)}) collective-permute-start(bf16[80,256]{1,0:T(8,128)(2,1)S(1)} %group_pass.1.own_ref), channel_id=1, source_target_pairs={{0,112},{16,0},{32,16},{48,32},{64,48},{80,64},{96,80},{112,96},{1... | collective-permute-start | bytes 122888 | tf_op jit(solution)/shard_map/ppermute | solution.py:447
  90.8 6.9 %collective-permute-start.13 = (bf16[80,256]{1,0:T(8,128)(2,1)S(1)}, bf16[80,256]{1,0:T(8,128)(2,1)S(1)}, u32[]{:S(2)}, u32[]{:S(2)}) collective-permute-start(bf16[80,256]{1,0:T(8,128)(2,1)S(1)} %group_pass.1.own_ref), channel_id=1, source_target_pairs={{0,96},{16,112},{32,0},{48,16},{64,32},{80,48},{96,64},{112,80},{1... | collective-permute-start | bytes 122888 | tf_op jit(solution)/shard_map/ppermute | solution.py:447
  91.5 56.7 %copy-start.2 = (bf16[4,256,256]{2,1,0:T(8,128)(2,1)S(1)}, bf16[4,256,256]{2,1,0:T(8,128)(2,1)}, u32[]{:S(2)}) copy-start(bf16[4,256,256]{2,1,0:T(8,128)(2,1)} %transfer_ref.3) | copy-start | bytes 1572868
  91.5 56.7 %copy-start.5 = (bf16[1,256,256]{2,1,0:T(8,128)(2,1)S(1)}, bf16[1,256,256]{2,1,0:T(8,128)(2,1)}, u32[]{:S(2)}) copy-start(bf16[1,256,256]{2,1,0:T(8,128)(2,1)} %node_transfer_ref.3) | copy-start | bytes 393220
  91.5 56.6 %collective-permute-start.12 = (bf16[80,256]{1,0:T(8,128)(2,1)S(1)}, bf16[80,256]{1,0:T(8,128)(2,1)S(1)}, u32[]{:S(2)}, u32[]{:S(2)}) collective-permute-start(bf16[80,256]{1,0:T(8,128)(2,1)S(1)} %group_pass.1.own_ref), channel_id=1, source_target_pairs={{0,80},{16,96},{32,112},{48,0},{64,16},{80,32},{96,48},{112,64},{1... | collective-permute-start | bytes 122888 | tf_op jit(solution)/shard_map/ppermute | solution.py:447
  91.5 56.6 %collective-permute-start.11 = (bf16[80,256]{1,0:T(8,128)(2,1)S(1)}, bf16[80,256]{1,0:T(8,128)(2,1)S(1)}, u32[]{:S(2)}, u32[]{:S(2)}) collective-permute-start(bf16[80,256]{1,0:T(8,128)(2,1)S(1)} %group_pass.1.own_ref), channel_id=1, source_target_pairs={{0,64},{16,80},{32,96},{48,112},{64,0},{80,16},{96,32},{112,48},{1... | collective-permute-start | bytes 122888 | tf_op jit(solution)/shard_map/ppermute | solution.py:447
  95.5 52.6 %collective-permute-start.10 = (bf16[80,256]{1,0:T(8,128)(2,1)S(1)}, bf16[80,256]{1,0:T(8,128)(2,1)S(1)}, u32[]{:S(2)}, u32[]{:S(2)}) collective-permute-start(bf16[80,256]{1,0:T(8,128)(2,1)S(1)} %group_pass.1.own_ref), channel_id=1, source_target_pairs={{0,48},{16,64},{32,80},{48,96},{64,112},{80,0},{96,16},{112,32},{1... | collective-permute-start | bytes 122888 | tf_op jit(solution)/shard_map/ppermute | solution.py:447
  95.5 52.6 %collective-permute-start.9 = (bf16[80,256]{1,0:T(8,128)(2,1)S(1)}, bf16[80,256]{1,0:T(8,128)(2,1)S(1)}, u32[]{:S(2)}, u32[]{:S(2)}) collective-permute-start(bf16[80,256]{1,0:T(8,128)(2,1)S(1)} %group_pass.1.own_ref), channel_id=1, source_target_pairs={{0,32},{16,48},{32,64},{48,80},{64,96},{80,112},{96,0},{112,16},{1... | collective-permute-start | bytes 122888 | tf_op jit(solution)/shard_map/ppermute | solution.py:447
  97.7 50.5 %collective-permute-start.8 = (bf16[80,256]{1,0:T(8,128)(2,1)S(1)}, bf16[80,256]{1,0:T(8,128)(2,1)S(1)}, u32[]{:S(2)}, u32[]{:S(2)}) collective-permute-start(bf16[80,256]{1,0:T(8,128)(2,1)S(1)} %group_pass.1.own_ref), channel_id=1, source_target_pairs={{0,16},{16,32},{32,48},{48,64},{64,80},{80,96},{96,112},{112,0},{1... | collective-permute-start | bytes 122888 | tf_op jit(solution)/shard_map/ppermute | solution.py:447
